TPU v7x, 128 devices: a whole 4x4x4 slice. The times are simulated.
128 devices in a mesh: expert: 16 (over y, z), etensor: 8 (over x, core).
Axes of the slice: x: 4, y: 4, z: 4, core: 2. Of those that a mesh axis runs over, the one named last changes fastest.
Arguments:
- tokens: bfloat16 [2048, 7168], P('expert', 'etensor'), may hold values from -6 to 6
- expert_ids: int32 [2048, 8], P('expert'), may hold values from 0 to 31, all different within a row; in each aligned block of 128 rows (0 to 127, 128 to 255, ...) at most 36 rows name the same one
- gate_weights: float32 [2048, 8], P('expert'), may hold values from 0.1 to 1
- gate_up: bfloat16 [32, 7168, 2, 2048], P('expert', None, None, 'etensor'), may hold values from -0.0625 to 0.0625
- down_proj: bfloat16 [32, 2048, 7168], P('expert', 'etensor'), may hold values from -0.125 to 0.125
Outputs:
- mixed: bfloat16 [2048, 7168], P('expert', 'etensor')
Inputs may be any that keep to these rules, and one draw needn't show every extreme that they name: `expert_ids`: each row names 8 different experts. Within each aligned block of 128 rows no expert is named by more than 36 rows, and in some block some expert is named by exactly 36 rows.
All inputs are finite; a program needn't handle non-finite values.
Results may differ from a plain program's by a relative error of at most 0.019.
Values may be sent and summed in bfloat16 or wider, within the bound.
A program may use at most 320 MiB of HBM per device.

v0:
```python
import jax
import jax.numpy as jnp
from jax import lax
from jax.sharding import PartitionSpec as P


def on_device(tokens, expert_ids, gate_weights, gate_up, down_proj):
    n_owner = lax.axis_size("expert")
    tok_dev = tokens.shape[0]
    top_k = expert_ids.shape[1]
    exp_dev = gate_up.shape[0]
    model_width = down_proj.shape[2]
    experts = exp_dev * n_owner
    capacity = 9 * tok_dev * top_k // (8 * experts)
    all_slots = experts * capacity
    per_owner = exp_dev * capacity
    flat_ids = expert_ids.reshape(-1)
    onehot = (flat_ids[:, None] == jnp.arange(experts, dtype=jnp.int32)[None, :]).astype(jnp.int32)
    earlier = jnp.cumsum(onehot, axis=0) - onehot
    position = jnp.sum(earlier * onehot, axis=1)
    slot_ids = (flat_ids * capacity + position).reshape(tok_dev, top_k)
    matches = slot_ids[:, :, None] == jnp.arange(all_slots, dtype=jnp.int32)[None, None, :]
    placing = jnp.sum(matches.astype(jnp.float32), axis=1).astype(jnp.bfloat16)
    full_tokens = lax.all_gather(tokens, "etensor", axis=1, tiled=True)
    placed = jnp.einsum("ts,td->sd", placing, full_tokens, preferred_element_type=jnp.float32)
    arrived = lax.all_to_all(
        placed.astype(jnp.bfloat16).reshape(n_owner, per_owner, full_tokens.shape[1]),
        "expert",
        split_axis=0,
        concat_axis=0,
        tiled=True,
    )
    row_block = arrived.reshape(n_owner, exp_dev, capacity, model_width)
    projected = jnp.einsum(
        "ojcd,jdgf->ojcgf", row_block, gate_up, preferred_element_type=jnp.float32
    )
    hidden = (jax.nn.silu(projected[:, :, :, 0, :]) * projected[:, :, :, 1, :]).astype(jnp.bfloat16)
    partial_value = jnp.einsum(
        "ojcf,jfd->ojcd", hidden, down_proj, preferred_element_type=jnp.float32
    )
    partial_value = partial_value.reshape(n_owner, per_owner, model_width)
    returned = lax.all_to_all(
        partial_value.astype(jnp.bfloat16), "expert", split_axis=0, concat_axis=0, tiled=True
    )
    returned = returned.reshape(all_slots, model_width)
    chosen = returned[slot_ids].astype(jnp.float32)
    gated = jnp.sum(chosen * gate_weights[:, :, None], axis=1)
    mixed = lax.psum_scatter(gated.astype(jnp.bfloat16), "etensor", scatter_dimension=1, tiled=True)
    return mixed


def solution(mesh):
    placed = (
        P("expert", "etensor"),
        P("expert", None),
        P("expert", None),
        P("expert", None, None, "etensor"),
        P("expert", "etensor", None),
    )
    return jax.shard_map(
        on_device, mesh=mesh, in_specs=placed, out_specs=P("expert", "etensor"), check_vma=False
    )
```

profile of v0, /device:TPU:1, one launch (start us, length us, event | category | flops | bytes accessed | tf_op | source)
XLA Modules:
  0.0 709.2 jit_solution(17228226124360600978)
XLA Ops:
  6.5 0.7 all-gather.2.cloned.1.call-update
  7.3 0.8 copy.49
  8.2 9.0 %reduce-window.6 = s32[32,8,128]{2,1,0:T(8,128)S(1)} reduce-window(s32[32,8,128]{2,1,0:T(8,128)S(1)} %fusion.14, s32[]{:T(128)} %constant.4.clone.1), window={size=1x1x128 pad=0_0x0_0x127_0}, to_apply=%region_0.0 | reduce-window | flops 4161536 | bytes 262148 | tf_op jit(solution)/shard_map/reduce-window
  17.4 0.1 copy.51
  17.6 0.1 broadcast_add_fusion
  17.9 0.7 compare_select_fusion
  18.6 0.1 copy.54
  18.7 1.5 convert_reduce_fusion
  20.2 17.6 %all-gather.2.cloned.1.call-done = bf16[128,7168]{1,0:T(8,128)(2,1)} async-done(((bf16[128,896]{1,0:T(8,128)(2,1)}), bf16[128,7168]{1,0:T(8,128)(2,1)}) %all-gather.2.cloned.1.call-update) | async-done | bytes 1835024 | tf_op jit(solution)/shard_map/all_gather | solution.py:24
  37.8 9.5 %convolution_convert_fusion = bf16[1152,7168]{1,0:T(8,128)(2,1)} fusion(bf16[128,7168]{1,0:T(8,128)(2,1)} %all-gather.2.cloned.1.call-done, bf16[128,1152]{1,0:T(8,128)(2,1)S(1)} %convert_reduce_fusion), kind=kOutput, calls=%fused_computation.3 | convolution fusion | flops 2122186752 | bytes 18644992 | tf_op jit(solution)/shard_map/ts,td->sd/dot_general | solution.py:25
  47.2 188.6 %all_to_all.10 = bf16[16,72,7168]{2,1,0:T(8,128)(2,1)S(1)} all-to-all(bf16[16,72,7168]{2,1,0:T(8,128)(2,1)} %bitcast.56), channel_id=1, replica_groups=mesh['expert'=16,'etensor'=8] {'expert'}, dimensions={0} | all-to-all | bytes 33030144 | tf_op jit(solution)/shard_map/all_to_all | solution.py:26
  235.9 25.3 %copy.55 = bf16[16,72,7168]{2,0,1:T(8,128)(2,1)} copy(bf16[16,72,7168]{2,1,0:T(8,128)(2,1)S(1)} %all_to_all.10) | data formatting | bytes 33030144 | tf_op jit(solution)/shard_map/all_to_all | solution.py:26
  261.1 14.4 %fusion.4 = f32[16,2,36,2,256]{4,0,3,2,1:T(8,128)S(1)} fusion(bf16[16,2,36,7168,1]{3,0,4,2,1:T(8,128)(2,1)} %bitcast.58, bf16[2,7168,2,256,1]{3,2,1,0,4:T(2,128)(2,1)} %bitcast.63), kind=kOutput, calls=%fused_computation.10 | convolution fusion | flops 8455716864 | bytes 33554432 | tf_op jit(solution)/shard_map/ojcd,jdgf->ojcgf/dot_general | solution.py:34
  275.5 0.4 fusion.8
  275.9 12.0 %convert_bitcast_fusion = bf16[16,2,36,7168]{3,2,0,1:T(8,128)(2,1)} fusion(bf16[2,256,7168]{2,1,0:T(8,128)(2,1)} %param.9, bf16[16,2,36,256]{3,0,2,1:T(8,128)(2,1)S(1)} %fusion.8), kind=kOutput, calls=%fused_computation.4 | convolution fusion | flops 4236115968 | bytes 24444928 | tf_op jit(solution)/shard_map/ojcf,jfd->ojcd/dot_general | solution.py:38
  287.9 12.3 %copy.59 = bf16[16,2,36,7168]{3,0,2,1:T(8,128)(2,1)S(1)} copy(bf16[16,2,36,7168]{3,2,0,1:T(8,128)(2,1)} %convert_bitcast_fusion) | data formatting | bytes 33030144 | tf_op jit(solution)/shard_map/convert_element_type | solution.py:43
  300.2 21.5 %copy.60 = bf16[16,72,7168]{2,1,0:T(8,128)(2,1)} copy(bf16[16,72,7168]{2,0,1:T(8,128)(2,1)S(1)} %bitcast.57) | data formatting | bytes 33030144 | tf_op jit(solution)/shard_map/convert_element_type | solution.py:43
  321.7 5.3 all-to-all-start.1
  327.3 288.4 %all-to-all-done.1 = bf16[16,72,7168]{2,1,0:T(8,128)(2,1)} async-done(((bf16[16,72,7168]{2,1,0:T(8,128)(2,1)}), bf16[16,72,7168]{2,1,0:T(8,128)(2,1)}, u32[]{:S(2)}, u32[]{:S(2)}) %all-to-all-start.1) | async-done | bytes 16515104 | tf_op jit(solution)/shard_map/all_to_all | solution.py:42
  615.7 32.6 %gather_fusion = bf16[1024,7168]{1,0:T(8,128)(2,1)} fusion(bf16[1152,7168]{1,0:T(8,128)(2,1)} %bitcast.14, s32[1024]{0:T(1024)S(1)} %broadcast_clamp_fusion), kind=kCustom, calls=%fused_computation | custom fusion | bytes 29364224 | tf_op jit(solution)/shard_map/gather | solution.py:46
  648.3 12.0 %fusion = bf16[128,7168]{1,0:T(8,128)(2,1)S(1)} fusion(bf16[1024,7168]{1,0:T(8,128)(2,1)} %gather_fusion, f32[128,8]{1,0:T(8,128)S(1)} %copy.62), kind=kLoop, calls=%fused_computation.2 | loop fusion | flops 21102592 | bytes 16519168 | tf_op jit(solution)/shard_map/reduce_sum | solution.py:47
  660.3 2.3 copy.68
  662.7 37.9 %reduce-scatter.4.cloned.1.call-done = bf16[896,128]{1,0:T(8,128)(2,1)} async-done(((bf16[7168,128]{1,0:T(8,128)(2,1)}), bf16[896,128]{1,0:T(8,128)(2,1)}) %reduce-scatter.4.cloned.1.call-update) | async-done | bytes 229392
  700.6 1.8 copy.69
  (19 shorter events, 0.9 us)
Async XLA Ops:
  6.5 31.2 %all-gather.2.cloned.1.call-start = ((), (), s32[]{:S(2)}) async-start(), calls=%async_computation.3 | async-start | bytes 2064384 | tf_op jit(solution)/shard_map/all_gather | solution.py:24
  321.7 5.5 copy-start
  321.7 294.0 %all-to-all-start.1 = ((bf16[16,72,7168]{2,1,0:T(8,128)(2,1)}), bf16[16,72,7168]{2,1,0:T(8,128)(2,1)}, u32[]{:S(2)}, u32[]{:S(2)}) async-start(bf16[16,72,7168]{2,1,0:T(8,128)(2,1)} %copy.60), calls=%async_computation.1 | async-start | bytes 33030144 | tf_op jit(solution)/shard_map/all_to_all | solution.py:42
  327.0 373.6 %reduce-scatter.4.cloned.1.call-start = ((), (), s32[]{:S(2)}) async-start(), calls=%async_computation.4 | async-start | bytes 2064384
Sparse Core Ops, SparseCore 0:
  9.1 28.6 all-gather.1
  662.8 37.7 reduce-scatter.3
where the time goes:
time: 712 us; the launch traced here: 709 us
  waiting for transfers between devices  345 us (48%)
  blocking collectives  189 us (27%)
  local copies, waits for them, and re-layouts  97.5 us (14%)
  matrix products  35.8 us (5%)
  other arithmetic  23.8 us (3%)
  between operations  13.5 us (2%)
    all_to_all x1, waiting for transfers between devices, on_device(): lax.all_to_all(partial_value.astype(jnp.bfloat16), 'expert', split_axis=0...  288 us
    all_to_all x1, blocking collectives, on_device(): lax.all_to_all(placed.astype(jnp.bfloat16).reshape(n_owner, per_owner, fu...  189 us
    unnamed x3, waiting for transfers between devices  38.6 us
    convert_element_type x2, local copies, waits for them, and re-layouts, on_device(): partial_value.astype(jnp.bfloat16)  33.8 us
    gather x1, local copies, waits for them, and re-layouts, on_device(): chosen = returned[slot_ids].astype(jnp.float32)  32.6 us
    all_to_all x1, local copies, waits for them, and re-layouts, on_device(): lax.all_to_all(placed.astype(jnp.bfloat16).reshape(n_owner, per_owner, fu...  25.3 us
    all_gather x1, waiting for transfers between devices, on_device(): full_tokens = lax.all_gather(tokens, 'etensor', axis=1, tiled=True)  17.6 us
    dot_general x1, matrix products, on_device(): jnp.einsum('ojcd,jdgf->ojcgf', row_block, gate_up, preferred_element_type...  14.4 us
  transfers between devices with their start and end apart: 3, of which 3 were waited for; matrix products, arithmetic and copies ran while one was open for 2% of the time, Pallas kernels for 0%

commit v1 on v0

v1 whole, which is shorter than its diff:
```python
import jax
import jax.numpy as jnp
from jax import lax
from jax.sharding import PartitionSpec as P


def on_device(tokens, expert_ids, gate_weights, gate_up, down_proj):
    n_owner = lax.axis_size("expert")
    n_shard = lax.axis_size("etensor")
    tok_dev, width = tokens.shape
    top_k = expert_ids.shape[1]
    exp_dev = gate_up.shape[0]
    experts = exp_dev * n_owner
    capacity = 9 * tok_dev * top_k // (8 * experts)
    all_slots = experts * capacity
    per_owner = exp_dev * capacity
    hits = expert_ids[:, :, None] == jnp.arange(experts, dtype=jnp.int32)
    named = jnp.sum(hits.astype(jnp.float32), axis=1)
    gates = jnp.sum(jnp.where(hits, gate_weights[:, :, None], 0.0), axis=1)
    rows = jnp.arange(tok_dev)
    before = (rows[None, :] < rows[:, None]).astype(jnp.float32)
    position = jnp.dot(before, named, preferred_element_type=jnp.float32)
    at_slot = (position[:, :, None] == jnp.arange(capacity, dtype=jnp.float32)) & (named[:, :, None] > 0)
    placing = at_slot.astype(jnp.bfloat16).reshape(tok_dev, all_slots)
    gate_hi = gates.astype(jnp.bfloat16)
    gate_lo = (gates - gate_hi.astype(jnp.float32)).astype(jnp.bfloat16)
    zero = jnp.zeros((), jnp.bfloat16)
    taking_hi = jnp.where(at_slot, gate_hi[:, :, None], zero).reshape(tok_dev, all_slots)
    taking_lo = jnp.where(at_slot, gate_lo[:, :, None], zero).reshape(tok_dev, all_slots)

    placed = jnp.einsum("ts,td->sd", placing, tokens, preferred_element_type=jnp.float32)
    arrived = lax.all_to_all(
        placed.astype(jnp.bfloat16).reshape(n_owner, per_owner, width),
        "expert",
        split_axis=0,
        concat_axis=0,
        tiled=True,
    )
    full = lax.all_gather(arrived, "etensor", axis=0, tiled=False)
    full = full.reshape(n_shard, n_owner, exp_dev, capacity, width)
    split_up = gate_up.reshape(exp_dev, n_shard, width, 2, gate_up.shape[3])
    projected = jnp.einsum(
        "sojcd,jsdgf->ojcgf", full, split_up, preferred_element_type=jnp.float32
    )
    hidden = (jax.nn.silu(projected[:, :, :, 0, :]) * projected[:, :, :, 1, :]).astype(jnp.bfloat16)
    split_down = down_proj.reshape(exp_dev, down_proj.shape[1], n_shard, width)
    partial_value = jnp.einsum(
        "ojcf,jfsd->sojcd", hidden, split_down, preferred_element_type=jnp.float32
    ).astype(jnp.bfloat16)
    summed = lax.psum_scatter(
        partial_value.reshape(n_shard, n_owner, per_owner, width),
        "etensor",
        scatter_dimension=0,
        tiled=False,
    )
    returned = lax.all_to_all(summed, "expert", split_axis=0, concat_axis=0, tiled=True)
    returned = returned.reshape(all_slots, width)
    mixed = jnp.dot(taking_hi, returned, preferred_element_type=jnp.float32)
    mixed = mixed + jnp.dot(taking_lo, returned, preferred_element_type=jnp.float32)
    return mixed.astype(jnp.bfloat16)


def solution(mesh):
    placed = (
        P("expert", "etensor"),
        P("expert", None),
        P("expert", None),
        P("expert", None, None, "etensor"),
        P("expert", "etensor", None),
    )
    return jax.shard_map(
        on_device, mesh=mesh, in_specs=placed, out_specs=P("expert", "etensor"), check_vma=False
    )
```

time: 712 us -> 312 us (0.44)
  blocking collectives: 189 us -> 34.6 us
  waiting for transfers between devices: 345 us -> 191 us
  local copies, waits for them, and re-layouts: 97.5 us -> 29.6 us
  other arithmetic: 23.8 us -> 1.39 us
    all_to_all x1, waiting for transfers between devices: 288 us -> 24.8 us  [on_device(): lax.all_to_all(summed, 'expert', split_axis=0, concat_axis=0, tiled=True)]
    all_to_all x1, blocking collectives: 189 us -> 34.6 us  [on_device(): lax.all_to_all(placed.astype(jnp.bfloat16).reshape(n_owner, per_owner, wi...]
    reduce_scatter x0 -> x1, waiting for transfers between devices: none -> 90.3 us  [on_device(): lax.psum_scatter(partial_value.reshape(n_shard, n_owner, per_owner, width...]
    all_gather x1, waiting for transfers between devices: 17.6 us -> 76.2 us  [on_device(): full = lax.all_gather(arrived, 'etensor', axis=0, tiled=False)]
    unnamed x3 -> x2, waiting for transfers between devices: 38.6 us -> 0.03 us
    gather x1 -> x0, local copies, waits for them, and re-layouts: 32.6 us -> none  [on_device(): chosen = returned[slot_ids].astype(jnp.float32)]
    all_to_all x1, local copies, waits for them, and re-layouts: 25.3 us -> 1.61 us  [on_device(): lax.all_to_all(placed.astype(jnp.bfloat16).reshape(n_owner, per_owner, wi...]
    convert_element_type x2 -> x1, local copies, waits for them, and re-layouts: 33.8 us -> 16 us  [on_device(): partial_value = jnp.einsum('ojcf,jfsd->sojcd', hidden, split_down, prefer...]
  transfers between devices with their start and end apart: 3 -> 3, of which waited for: 3 -> 3; matrix products, arithmetic and copies ran while one was open for 2% -> 3% of each run, Pallas kernels for 0% -> 0%
where the time goes in v1:
time: 312 us; the launch traced here: 308 us
  waiting for transfers between devices  191 us (61%)
  blocking collectives  34.6 us (11%)
  matrix products  30.7 us (10%)
  local copies, waits for them, and re-layouts  29.6 us (9%)
  between operations  13.5 us (4%)
  starting transfers between devices  6.74 us (2%)
    reduce_scatter x1, waiting for transfers between devices, on_device(): lax.psum_scatter(partial_value.reshape(n_shard, n_owner, per_owner, width...  90.3 us
    all_gather x1, waiting for transfers between devices, on_device(): full = lax.all_gather(arrived, 'etensor', axis=0, tiled=False)  76.2 us
    all_to_all x1, blocking collectives, on_device(): lax.all_to_all(placed.astype(jnp.bfloat16).reshape(n_owner, per_owner, wi...  34.6 us
    all_to_all x1, waiting for transfers between devices, on_device(): lax.all_to_all(summed, 'expert', split_axis=0, concat_axis=0, tiled=True)  24.8 us
    convert_element_type x1, local copies, waits for them, and re-layouts, on_device(): partial_value = jnp.einsum('ojcf,jfsd->sojcd', hidden, split_down, prefer...  16 us
    dot_general x1, matrix products, on_device(): jnp.einsum('sojcd,jsdgf->ojcgf', full, split_up, preferred_element_type=j...  14.4 us
    dot_general x1, matrix products, on_device(): jnp.einsum('ojcf,jfsd->sojcd', hidden, split_down, preferred_element_type...  13.7 us
    all_to_all x1, starting transfers between devices, on_device(): lax.all_to_all(summed, 'expert', split_axis=0, concat_axis=0, tiled=True)  6.7 us
  transfers between devices with their start and end apart: 3, of which 3 were waited for; matrix products, arithmetic and copies ran while one was open for 3% of the time, Pallas kernels for 0%

profile of v1, /device:TPU:1, one launch (start us, length us, event | category | flops | bytes accessed | tf_op | source)
XLA Modules:
  0.0 307.9 jit_solution(9634713113643978393)
XLA Ops:
  6.5 0.8 select_reduce_fusion
  7.3 0.1 fusion.17
  7.5 0.1 eq.61
  7.7 0.1 and.31
  7.8 0.7 convolution_convert_fusion
  8.6 34.6 %all_to_all.10 = bf16[16,72,896]{2,1,0:T(8,128)(2,1)S(1)} all-to-all(bf16[16,72,896]{2,1,0:T(8,128)(2,1)S(1)} %bitcast.64), channel_id=1, replica_groups=mesh['expert'=16,'etensor'=8] {'expert'}, dimensions={0} | all-to-all | bytes 4128768 | tf_op jit(solution)/shard_map/all_to_all | solution.py:32
  43.2 1.6 copy.38
  44.8 0.0 reduce-scatter.2.cloned.1.call-start
  44.8 4.8 %copy.57 = bf16[64,8,8,896]{3,2,1,0:T(8,128)(2,1)S(1)} copy(bf16[64,8,8,896]{3,1,2,0:T(8,128)(2,1)} %bitcast.65) | data formatting | bytes 14680064
  49.6 3.6 %bitcast_bitcast_fusion = bf16[2,256,8,896,1]{3,2,1,0,4:T(8,128)(2,1)} fusion(bf16[2,256,8,896]{3,2,1,0:T(8,128)(2,1)S(1)} %bitcast.61), kind=kLoop, calls=%fused_computation.3 | loop fusion | bytes 14680064 | tf_op jit(solution)/shard_map/reshape | solution.py:46
  53.2 76.2 %all-gather.3.cloned.1.call-done = bf16[128,72,896]{2,0,1:T(8,128)(2,1)} async-done(((bf16[16,72,896]{2,0,1:T(8,128)(2,1)}), bf16[128,72,896]{2,0,1:T(8,128)(2,1)}) %all-gather.3.cloned.1.call-update) | async-done | bytes 16515088 | tf_op jit(solution)/shard_map/all_gather | solution.py:39
  129.4 14.4 %fusion.3 = f32[16,2,36,2,256]{4,0,3,2,1:T(8,128)S(1)} fusion(bf16[8,16,2,36,896,1]{4,1,0,5,3,2:T(8,128)(2,1)} %bitcast.67, bf16[2,8,896,2,256,1]{4,3,2,1,0,5:T(2,128)(2,1)} %bitcast.68), kind=kOutput, calls=%fused_computation.6 | convolution fusion | flops 8455716864 | bytes 33554432 | tf_op jit(solution)/shard_map/sojcd,jsdgf->ojcgf/dot_general | solution.py:42
  143.8 0.4 fusion.15
  144.2 13.7 %convert_bitcast_fusion = bf16[8,16,2,36,896]{4,3,0,1,2:T(8,128)(2,1)} fusion(bf16[2,256,8,896,1]{3,2,1,0,4:T(8,128)(2,1)} %bitcast_bitcast_fusion, bf16[16,2,36,256,1]{3,0,2,1,4:T(8,128)(2,1)S(1)} %fusion.15), kind=kOutput, calls=%fused_computation | convolution fusion | flops 4236115968 | bytes 24444928 | tf_op jit(solution)/shard_map/ojcf,jfsd->sojcd/dot_general | solution.py:47
  157.8 16.0 %copy.43 = bf16[8,16,2,36,896]{4,1,3,2,0:T(8,128)(2,1)} copy(bf16[8,16,2,36,896]{4,3,0,1,2:T(8,128)(2,1)} %convert_bitcast_fusion) | data formatting | bytes 33030144 | tf_op jit(solution)/shard_map/convert_element_type | solution.py:49
  173.8 90.3 %reduce-scatter.2.cloned.1.call-done = bf16[1,16,72,896]{3,1,2,0:T(8,128)(2,1)} async-done(((bf16[8,16,72,896]{3,1,2,0:T(8,128)(2,1)}), bf16[1,16,72,896]{3,1,2,0:T(8,128)(2,1)}) %reduce-scatter.2.cloned.1.call-update) | async-done | bytes 2064400 | tf_op jit(solution)/shard_map/reduce_scatter | solution.py:50
  264.1 3.3 %copy.44 = bf16[16,72,896]{2,1,0:T(8,128)(2,1)} copy(bf16[16,72,896]{2,0,1:T(8,128)(2,1)} %bitcast.66) | data formatting | bytes 4128768 | tf_op jit(solution)/shard_map/reduce_scatter | solution.py:50
  267.4 6.7 %all-to-all-start.1 = ((bf16[16,72,896]{2,1,0:T(8,128)(2,1)}), bf16[16,72,896]{2,1,0:T(8,128)(2,1)S(1)}, u32[]{:S(2)}, u32[]{:S(2)}) async-start(bf16[16,72,896]{2,1,0:T(8,128)(2,1)} %copy.44), calls=%async_computation.2 | async-start | bytes 4128768 | tf_op jit(solution)/shard_map/all_to_all | solution.py:56
  274.1 0.2 fusion.11
  274.3 0.1 select_n.35
  274.4 0.1 select_n.33
  274.5 24.8 %all-to-all-done.1 = bf16[16,72,896]{2,1,0:T(8,128)(2,1)S(1)} async-done(((bf16[16,72,896]{2,1,0:T(8,128)(2,1)}), bf16[16,72,896]{2,1,0:T(8,128)(2,1)S(1)}, u32[]{:S(2)}, u32[]{:S(2)}) %all-to-all-start.1) | async-done | bytes 2064416 | tf_op jit(solution)/shard_map/all_to_all | solution.py:56
  299.3 0.5 fusion.18
  299.8 1.2 fusion.6
  (13 shorter events, 0.2 us)
Async XLA Ops:
  6.5 1.3 copy-start
  6.5 122.8 %all-gather.3.cloned.1.call-start = ((), (), s32[]{:S(2)}) async-start(), calls=%async_computation.4 | async-start | bytes 18579456 | tf_op jit(solution)/shard_map/all_gather | solution.py:39
  44.8 219.3 %reduce-scatter.2.cloned.1.call-start = ((), (), s32[]{:S(2)}) async-start(), calls=%async_computation.3 | async-start | bytes 18579456 | tf_op jit(solution)/shard_map/reduce_scatter | solution.py:50
  267.4 31.9 %all-to-all-start.1 = ((bf16[16,72,896]{2,1,0:T(8,128)(2,1)}), bf16[16,72,896]{2,1,0:T(8,128)(2,1)S(1)}, u32[]{:S(2)}, u32[]{:S(2)}) async-start(bf16[16,72,896]{2,1,0:T(8,128)(2,1)} %copy.44), calls=%async_computation.2 | async-start | bytes 4128768 | tf_op jit(solution)/shard_map/all_to_all | solution.py:56
  299.3 1.8 copy-start.1
Sparse Core Ops, SparseCore 0:
  44.9 84.4 all-gather.2
  173.9 90.1 reduce-scatter.1

commit v2 on v0

v2 whole, which is shorter than its diff:
```python
import jax
import jax.numpy as jnp
from jax import lax
from jax.experimental import pallas as pl
from jax.experimental.pallas import tpu as pltpu
from jax.sharding import PartitionSpec as P

MESH = pl.DeviceIdType.MESH
F32, BF16 = jnp.float32, jnp.bfloat16
N = 4
SUB = 48


def dot(a, b):
    return jnp.dot(a, b, preferred_element_type=F32)


def kernel(cap, tokens, route, gate_up, down, out, X, SB, OP, IN, RET, PL, T, RT, ZR, CB, ACC, HID, SLOT, GATE,
           WG, WD, wsem, ssem, rsem):
    half = N * cap
    rows = 2 * half
    top = route.shape[0] // 2
    tok, width = tokens.shape
    ff = down.shape[1]
    e, s = lax.axis_index("expert"), lax.axis_index("etensor")
    y, z, x, c = e // N, e % N, s // 2, s % 2

    def at_x(p, other):
        chip = (x + (0, N - 1, 1, 2)[p]) % N
        return chip * 2 + (1 - c if other else c)

    own, left, right, sibling = (e, s), (e, at_x(1, False)), (e, at_x(2, False)), (e, at_x(0, True))
    z_up = [(y * N + (z + d) % N, s) for d in range(N)]
    z_down = [(y * N + (z + N - d) % N, s) for d in range(N)]
    y_up = [((y + d) % N * N + z, s) for d in range(N)]
    y_down = [((y + N - d) % N * N + z, s) for d in range(N)]

    loads = []
    for q in range(2 * N):
        col = pl.multiple_of(at_x(q % N, q >= N) * width, 128)
        loads.append(pltpu.make_async_copy(gate_up.at[:, pl.ds(col, width), :], WG.at[q], wsem.at[2 * q]))
        loads.append(pltpu.make_async_copy(down.at[:, :, pl.ds(col, width)], WD.at[q], wsem.at[2 * q + 1]))
    for load in loads:
        load.start()

    barrier = pltpu.get_barrier_semaphore()
    friends = z_up[1:] + y_up[1:] + [left, right, sibling]
    for f in friends:
        pl.semaphore_signal(barrier, inc=1, device_id=f, device_id_type=MESH)
    pl.semaphore_wait(barrier, len(friends))

    copies = {}

    def plan(key, src, dst, device):
        i = len(copies)
        copies[key] = pltpu.make_async_remote_copy(
            src_ref=src, dst_ref=dst, send_sem=ssem.at[i], recv_sem=rsem.at[i], device_id=device, device_id_type=MESH
        )

    lo, hi = pl.ds(0, half), pl.ds(half, half)
    for d in range(1, N):
        plan(("zt", d), tokens, T.at[d], z_up[d])
        plan(("zr", d), route, RT.at[d], z_up[d])
        plan(("zo", d), T.at[d], ZR.at[d - 1], z_down[d])
        plan(("yt", d), PL.at[d - 1], X.at[0, d], y_up[d])
        plan(("yo", d), X.at[0, d], RET.at[d], y_down[d])
    for g in range(N):
        plan(("r", g), X.at[0, g], X.at[1, g], right)
        plan(("l", g), X.at[0, g], X.at[2, g], left)
        plan(("rr", g), X.at[1, g, lo], X.at[3, g, lo], right)
        plan(("ll", g), X.at[2, g, hi], X.at[3, g, hi], left)
        for p in range(N):
            plan(("s", g, p), X.at[p, g], X.at[N + p, g], sibling)
        plan(("S", g), X.at[pl.ds(N, N), g], SB.at[:, g], sibling)
        plan(("or", g), X.at[3, g, lo], OP.at[0, g], right)
        plan(("ol", g), X.at[3, g, hi], OP.at[1, g], left)
        plan(("ir", g, 0), X.at[2, g, hi], IN.at[0, g, hi], right)
        plan(("il", g, 0), X.at[1, g, lo], IN.at[1, g, lo], left)
        plan(("ir", g, 1), X.at[2, g, lo], IN.at[0, g, lo], right)
        plan(("il", g, 1), X.at[1, g, hi], IN.at[1, g, hi], left)

    def start(*key):
        copies[key].start()

    def sent(*key):
        copies[key].wait_send()

    def got(*key):
        copies[key].wait_recv()

    for d in (1, 3, 2):
        start("zr", d)
        start("zt", d)

    T[0] = tokens[...]
    RT[0] = route[...]

    line = lax.broadcasted_iota(jnp.int32, (2 * N, tok), 0)
    expert = (2 * (N * ((y + line // 2) % N) + z) + line % 2).astype(F32)
    before = lax.broadcasted_iota(jnp.int32, (tok, tok), 0) < lax.broadcasted_iota(jnp.int32, (tok, tok), 1)
    before = jnp.where(before, 1.0, 0.0).astype(BF16)
    for d in range(N):
        if d:
            got("zr", d)
        named = jnp.zeros((2 * N, tok), F32)
        gate = jnp.zeros((2 * N, tok), F32)
        for k in range(top):
            hit = RT[d, k : k + 1, :] == expert
            named = named + jnp.where(hit, 1.0, 0.0)
            gate = gate + jnp.where(hit, RT[d, top + k : top + k + 1, :], 0.0)
        position = dot(named.astype(BF16), before)
        SLOT[:, d * tok : (d + 1) * tok] = jnp.where(named > 0.0, position + float(d * cap), -1.0)
        GATE[:, d * tok : (d + 1) * tok] = gate

    slot_of = lax.broadcasted_iota(jnp.int32, (half, N * tok), 0).astype(F32)

    def place(g, to):
        for j in range(2):
            i = 2 * g + j
            takes = jnp.where(slot_of == SLOT[i : i + 1, :], 1.0, 0.0).astype(BF16)
            to[j * half : (j + 1) * half, :] = dot(takes, T[...].reshape(N * tok, width)).astype(BF16)

    for d in range(1, N):
        got("zt", d)

    place(0, X.at[0, 0])

    def stage_a(g):
        if g:
            got("yt", g)
        start("r", g)
        start("l", g)
        start("s", g, 0)

    stage_a(0)
    for g in (1, 3, 2):
        place(g, PL.at[g - 1])
        start("yt", g)

    def stage_b(g):
        got("r", g)
        start("rr", g)
        got("l", g)
        start("ll", g)
        start("s", g, 1)
        start("s", g, 2)

    def stage_c(g):
        got("rr", g)
        got("ll", g)
        start("s", g, 3)

    def stage_d(g):
        for p in range(N):
            got("s", g, p)
        ACC[...] = jnp.zeros_like(ACC)

        @pl.loop(0, 2 * N)
        def _(q):
            for j in range(2):
                piece = pl.ds(j * half, half)
                ACC[piece, :] += dot(X[q, g, piece, :], WG[q, j])

        a = ACC[...]
        HID[...] = (jax.nn.silu(a[:, :ff]) * a[:, ff:]).astype(BF16)

        def down_of(q):
            for j in range(2):
                piece = pl.ds(j * half, half)
                X[q, g, piece, :] = dot(HID[piece, :], WD[q, j]).astype(BF16)

        pl.loop(N, 2 * N)(down_of)
        start("S", g)
        for k in ("r", "l", "rr", "ll"):
            sent(k, g)
        for p in range(N):
            sent("s", g, p)
        pl.loop(0, N)(down_of)

    def add(n, to, terms):
        @pl.loop(0, n // SUB)
        def _(i):
            at = pl.ds(pl.multiple_of(i * SUB, SUB), SUB)
            total = terms[0][at, :].astype(F32)
            for t in terms[1:]:
                total = total + t[at, :].astype(F32)
            to[at, :] = total.astype(BF16)

    def stage_e(g):
        got("S", g)
        add(rows, X.at[3, g], [X.at[3, g], SB.at[3, g]])
        start("or", g)
        start("ol", g)
        add(half, X.at[2, g, hi], [X.at[2, g, hi], SB.at[2, g, hi]])
        start("ir", g, 0)
        add(half, X.at[1, g, lo], [X.at[1, g, lo], SB.at[1, g, lo]])
        start("il", g, 0)

    def stage_f(g):
        got("or", g)
        add(half, X.at[2, g, lo], [X.at[2, g, lo], SB.at[2, g, lo], OP.at[0, g]])
        start("ir", g, 1)
        got("ol", g)
        add(half, X.at[1, g, hi], [X.at[1, g, hi], SB.at[1, g, hi], OP.at[1, g]])
        start("il", g, 1)

    def stage_g(g):
        for k in range(2):
            got("ir", g, k)
            got("il", g, k)
        add(rows, X.at[0, g] if g else RET.at[0], [X.at[0, g], SB.at[0, g], IN.at[0, g], IN.at[1, g]])
        if g:
            start("yo", g)

    def stage_h(g):
        if g:
            got("yo", g)
        for j in range(2):
            i = 2 * g + j
            takes = jnp.where(slot_of == SLOT[i : i + 1, :], GATE[i : i + 1, :], 0.0).astype(BF16)
            product = lax.dot_general(
                takes, RET[g, j * half : (j + 1) * half, :], (((0,), (0,)), ((), ())), preferred_element_type=F32
            )
            CB[...] = product if i == 0 else CB[...] + product

    stage_a(1)
    stage_b(0)
    stage_a(2)
    stage_b(1)
    for d in loads:
        d.wait()
    stage_c(0)
    stage_d(0)
    stage_a(3)
    stage_b(2)
    stage_e(0)
    stage_c(1)
    stage_d(1)
    stage_f(0)
    stage_b(3)
    stage_e(1)
    stage_c(2)
    stage_d(2)
    stage_g(0)
    stage_f(1)
    stage_e(2)
    stage_c(3)
    stage_d(3)
    stage_g(1)
    stage_f(2)
    stage_e(3)
    stage_h(0)
    stage_h(1)
    stage_g(2)
    stage_f(3)
    stage_h(2)
    stage_g(3)
    stage_h(3)
    for d in range(1, N):
        sent("zt", d)
        T[d] = CB[d * tok : (d + 1) * tok, :].astype(BF16)
        start("zo", d)
    total = CB[0:tok, :]
    for d in range(1, N):
        got("zo", d)
        total = total + ZR[d - 1].astype(F32)
    out[...] = total.astype(BF16)

    for d in range(1, N):
        for k in ("zr", "zo", "yt", "yo"):
            sent(k, d)
    for g in range(N):
        sent("S", g)
        sent("or", g)
        sent("ol", g)
        for k in range(2):
            sent("ir", g, k)
            sent("il", g, k)


def on_device(tokens, expert_ids, gate_weights, gate_up, down_proj):
    tok, width = tokens.shape
    top = expert_ids.shape[1]
    exp_dev, deep, _, ff = gate_up.shape
    cap = 9 * tok * top // (8 * exp_dev * N * N)
    half = N * cap
    rows = exp_dev * half
    route = jnp.concatenate([expert_ids.T.astype(F32), gate_weights.T], axis=0)
    flops = 2 * N * rows * deep * ff * 3
    n_copies = 5 * (N - 1) + 15 * N
    return pl.pallas_call(
        lambda *refs: kernel(cap, *refs),
        out_shape=jax.ShapeDtypeStruct((tok, width), BF16),
        in_specs=[pl.BlockSpec(memory_space=pltpu.VMEM)] * 2 + [pl.BlockSpec(memory_space=pl.ANY)] * 2,
        out_specs=pl.BlockSpec(memory_space=pltpu.VMEM),
        scratch_shapes=[
            pltpu.VMEM((2 * N, N, rows, width), BF16),
            pltpu.VMEM((N, N, rows, width), BF16),
            pltpu.VMEM((2, N, half, width), BF16),
            pltpu.VMEM((2, N, rows, width), BF16),
            pltpu.VMEM((N, rows, width), BF16),
            pltpu.VMEM((N - 1, rows, width), BF16),
            pltpu.VMEM((N, tok, width), BF16),
            pltpu.VMEM((N, 2 * top, tok), F32),
            pltpu.VMEM((N - 1, tok, width), BF16),
            pltpu.VMEM((N * tok, width), F32),
            pltpu.VMEM((rows, 2 * ff), F32),
            pltpu.VMEM((rows, ff), BF16),
            pltpu.VMEM((2 * N, N * tok), F32),
            pltpu.VMEM((2 * N, N * tok), F32),
            pltpu.VMEM((2 * N, exp_dev, width, 2 * ff), BF16),
            pltpu.VMEM((2 * N, exp_dev, ff, width), BF16),
            pltpu.SemaphoreType.DMA((4 * N,)),
            pltpu.SemaphoreType.DMA((n_copies,)),
            pltpu.SemaphoreType.DMA((n_copies,)),
        ],
        compiler_params=pltpu.CompilerParams(
            collective_id=0, has_side_effects=True, vmem_limit_bytes=60 << 20
        ),
        cost_estimate=pl.CostEstimate(flops=flops, bytes_accessed=24 << 20, transcendentals=0),
    )(tokens, route, gate_up.reshape(exp_dev, deep, 2 * ff), down_proj)


def solution(mesh):
    placed = (
        P("expert", "etensor"),
        P("expert", None),
        P("expert", None),
        P("expert", None, None, "etensor"),
        P("expert", "etensor", None),
    )
    return jax.shard_map(
        on_device, mesh=mesh, in_specs=placed, out_specs=P("expert", "etensor"), check_vma=False
    )
```

time: 712 us -> 209 us (0.29)
  waiting for transfers between devices: 345 us -> 0 us
  blocking collectives: 189 us -> 0 us
  Pallas kernels: 0 us -> 180 us
  local copies, waits for them, and re-layouts: 97.5 us -> 25.3 us
  matrix products: 35.8 us -> 0 us
  other arithmetic: 23.8 us -> 1.97 us
  between operations: 13.5 us -> 0.01 us
    all_to_all x1 -> x0, waiting for transfers between devices: 288 us -> none  [on_device(): lax.all_to_all(partial_value.astype(jnp.bfloat16), 'expert', split_axis=0...]
    all_to_all x1 -> x0, blocking collectives: 189 us -> none  [on_device(): lax.all_to_all(placed.astype(jnp.bfloat16).reshape(n_owner, per_owner, fu...]
    pallas_call x0 -> x1, Pallas kernels: none -> 180 us  [on_device(): pl.pallas_call(lambda *refs: kernel(cap, *refs), out_shape=jax.ShapeDtype...]
    unnamed x3 -> x0, waiting for transfers between devices: 38.6 us -> none
    dot_general x3 -> x0, matrix products: 35.8 us -> none  [the longest x1 14.4 us: on_device(): jnp.einsum('ojcd,jdgf->ojcgf', row_block, gate_up, preferred_element_type...]
    convert_element_type x2 -> x0, local copies, waits for them, and re-layouts: 33.8 us -> none  [on_device(): partial_value.astype(jnp.bfloat16)]
    gather x1 -> x0, local copies, waits for them, and re-layouts: 32.6 us -> none  [on_device(): chosen = returned[slot_ids].astype(jnp.float32)]
    all_to_all x1 -> x0, local copies, waits for them, and re-layouts: 25.3 us -> none  [on_device(): lax.all_to_all(placed.astype(jnp.bfloat16).reshape(n_owner, per_owner, fu...]
  transfers between devices with their start and end apart: 3 -> 0, of which waited for: 3 -> 0; matrix products, arithmetic and copies ran while one was open for 2% -> 0% of each run, Pallas kernels for 0% -> 0%
where the time goes in v2:
time: 209 us; the launch traced here: 207 us
  Pallas kernels  180 us (86%)
  local copies, waits for them, and re-layouts  25.3 us (12%)
    pallas_call x1, Pallas kernels, on_device(): pl.pallas_call(lambda *refs: kernel(cap, *refs), out_shape=jax.ShapeDtype...  180 us
    reshape x1, local copies, waits for them, and re-layouts, on_device(): gate_up.reshape(exp_dev, deep, 2 * ff)  23.7 us

profile of v2, /device:TPU:1, one launch (start us, length us, event | category | flops | bytes accessed | tf_op | source)
XLA Modules:
  0.0 207.0 jit_solution(13144677702840505945)
XLA Ops:
  0.0 0.7 convert_bitcast_fusion
  0.7 1.3 pad_maximum_fusion.refs_1_
  2.0 23.7 %reshape.3.refs_2_ = bf16[2,7168,512]{2,1,0:T(8,128)(2,1)} reshape(bf16[2,7168,2,256]{3,2,1,0:T(2,128)(2,1)} %param.8) | data formatting | bytes 29360128 | tf_op jit(solution)/shard_map/reshape | solution.py:321
  25.6 179.7 %shard_map.55 = bf16[128,896]{1,0:T(8,128)(2,1)} custom-call(bf16[128,896]{1,0:T(8,128)(2,1)} %refs_0_.1, f32[16,128]{1,0:T(8,128)} %pad_maximum_fusion.refs_1_, bf16[2,7168,512]{2,1,0:T(8,128)(2,1)} %reshape.3.refs_2_, bf16[2,256,7168]{2,1,0:T(8,128)(2,1)} %refs_3_.1), custom_call_target="tpu_custom_call" | custom-call | flops 12683575296 | bytes 25165824 | tf_op jit(solution)/shard_map/pallas_call | solution.py:291
  205.4 1.6 copy.7

commit v3 on v2

--- a/solution.py
+++ b/solution.py
@@ -16,7 +16,7 @@
 
 
 def kernel(cap, tokens, route, gate_up, down, out, X, SB, OP, IN, RET, PL, T, RT, ZR, CB, ACC, HID, SLOT, GATE,
-           WG, WD, wsem, ssem, rsem):
+           WG, WD, STAGE, wsem, gsem, ssem, rsem):
     half = N * cap
     rows = 2 * half
     top = route.shape[0] // 2
@@ -38,10 +38,28 @@
     loads = []
     for q in range(2 * N):
         col = pl.multiple_of(at_x(q % N, q >= N) * width, 128)
-        loads.append(pltpu.make_async_copy(gate_up.at[:, pl.ds(col, width), :], WG.at[q], wsem.at[2 * q]))
-        loads.append(pltpu.make_async_copy(down.at[:, :, pl.ds(col, width)], WD.at[q], wsem.at[2 * q + 1]))
+        loads.append(pltpu.make_async_copy(down.at[:, :, pl.ds(col, width)], WD.at[q], wsem.at[q]))
     for load in loads:
         load.start()
+
+    def stage_in(n):
+        col = pl.multiple_of(at_x(n // 2 % N, n >= 2 * N) * width, 128)
+        return pltpu.make_async_copy(gate_up.at[n % 2, pl.ds(col, width)], STAGE.at[n % 2], gsem.at[n % 2])
+
+    def weights(first, last):
+        for n in range(first, last):
+            stage_in(n).wait()
+
+            @pl.loop(0, width // tok)
+            def _(i):
+                at = pl.ds(pl.multiple_of(i * tok, tok), tok)
+                WG[n // 2, n % 2, at, :] = STAGE[n % 2, at].reshape(tok, 2 * ff)
+
+            if n + 2 < 4 * N:
+                stage_in(n + 2).start()
+
+    stage_in(0).start()
+    stage_in(1).start()
 
     barrier = pltpu.get_barrier_semaphore()
     friends = z_up[1:] + y_up[1:] + [left, right, sibling]
@@ -120,6 +138,7 @@
             takes = jnp.where(slot_of == SLOT[i : i + 1, :], 1.0, 0.0).astype(BF16)
             to[j * half : (j + 1) * half, :] = dot(takes, T[...].reshape(N * tok, width)).astype(BF16)
 
+    weights(0, 6)
     for d in range(1, N):
         got("zt", d)
 
@@ -223,12 +242,16 @@
             )
             CB[...] = product if i == 0 else CB[...] + product
 
+    weights(6, 9)
     stage_a(1)
+    weights(9, 12)
     stage_b(0)
+    weights(12, 14)
     stage_a(2)
+    weights(14, 16)
     stage_b(1)
-    for d in loads:
-        d.wait()
+    for load in loads:
+        load.wait()
     stage_c(0)
     stage_d(0)
     stage_a(3)
@@ -310,15 +333,17 @@
             pltpu.VMEM((2 * N, N * tok), F32),
             pltpu.VMEM((2 * N, exp_dev, width, 2 * ff), BF16),
             pltpu.VMEM((2 * N, exp_dev, ff, width), BF16),
-            pltpu.SemaphoreType.DMA((4 * N,)),
+            pltpu.VMEM((2, width, 2, ff), BF16),
+            pltpu.SemaphoreType.DMA((2 * N,)),
+            pltpu.SemaphoreType.DMA((2,)),
             pltpu.SemaphoreType.DMA((n_copies,)),
             pltpu.SemaphoreType.DMA((n_copies,)),
         ],
         compiler_params=pltpu.CompilerParams(
-            collective_id=0, has_side_effects=True, vmem_limit_bytes=60 << 20
+            collective_id=0, has_side_effects=True, vmem_limit_bytes=62 << 20
         ),
         cost_estimate=pl.CostEstimate(flops=flops, bytes_accessed=24 << 20, transcendentals=0),
-    )(tokens, route, gate_up.reshape(exp_dev, deep, 2 * ff), down_proj)
+    )(tokens, route, gate_up, down_proj)
 
 
 def solution(mesh):

time: 209 us -> 186 us (0.89)
  local copies, waits for them, and re-layouts: 25.3 us -> 1.65 us
    reshape x1 -> x0, local copies, waits for them, and re-layouts: 23.7 us -> none  [on_device(): gate_up.reshape(exp_dev, deep, 2 * ff)]
    pallas_call x1, Pallas kernels: 180 us -> 182 us  [on_device(): pl.pallas_call(lambda *refs: kernel(cap, *refs), out_shape=jax.ShapeDtype...]
where the time goes in v3:
time: 186 us
  Pallas kernels  182 us (98%)
  other arithmetic  1.97 us (1%)
    pallas_call x1, Pallas kernels, on_device(): pl.pallas_call(lambda *refs: kernel(cap, *refs), out_shape=jax.ShapeDtype...  182 us

profile of v3, /device:TPU:1, one launch (start us, length us, event | category | flops | bytes accessed | tf_op | source)
XLA Modules:
  0.0 185.9 jit_solution(5499215229670673107)
XLA Ops:
  0.0 0.7 convert_bitcast_fusion
  0.7 1.3 pad_maximum_fusion.refs_1_
  2.0 182.2 %shard_map.55 = bf16[128,896]{1,0:T(8,128)(2,1)} custom-call(bf16[128,896]{1,0:T(8,128)(2,1)} %refs_0_.1, f32[16,128]{1,0:T(8,128)} %pad_maximum_fusion.refs_1_, bf16[2,7168,2,256]{3,2,1,0:T(2,128)(2,1)} %refs_2_.1, bf16[2,256,7168]{2,1,0:T(8,128)(2,1)} %refs_3_.1), custom_call_target="tpu_custom_call" | custom-call | flops 12683575296 | bytes 25165824 | tf_op jit(solution)/shard_map/pallas_call | solution.py:314
  184.2 1.6 copy.7

commit v4 on v3

v4 whole, which is shorter than its diff:
```python
import jax
import jax.numpy as jnp
from jax import lax
from jax.experimental import pallas as pl
from jax.experimental.pallas import tpu as pltpu
from jax.sharding import PartitionSpec as P

MESH = pl.DeviceIdType.MESH
F32, BF16 = jnp.float32, jnp.bfloat16
N = 4
SUB = 48


def dot(a, b):
    return jnp.dot(a, b, preferred_element_type=F32)


def kernel(cap, a_cols, tokens, ids, gates, gate_up, down, out, XA, XB, SA, SB, OP, IN, PL, PA, T, TA, RT, ZR, ZA, XR, CB, CA, ACC, HID,
           SLOT, GATE, WG, WD, STAGE, free, wsem, gsem, ssem, rsem):
    half = N * cap
    rows = 2 * half
    top = ids.shape[0]
    tok, width = tokens.shape
    ff = down.shape[1]
    e, s = lax.axis_index("expert"), lax.axis_index("etensor")
    y, z, x, c = e // N, e % N, s // 2, s % 2
    A, B = pl.ds(0, a_cols), pl.ds(a_cols, width - a_cols)
    lo, hi = pl.ds(0, half), pl.ds(half, half)
    here, there = pl.ds(0, N), pl.ds(N, N)

    def at_x(p, other):
        chip = (x + (0, N - 1, 1, 2)[p]) % N
        return chip * 2 + (1 - c if other else c)

    x_at = [(e, at_x(p, False)) for p in range(N)]
    back = (0, 2, 1, 3)
    left, right, sibling = x_at[1], x_at[2], (e, at_x(0, True))
    z_up = [(y * N + (z + d) % N, s) for d in range(N)]
    z_down = [(y * N + (z + N - d) % N, s) for d in range(N)]
    y_up = [((y + d) % N * N + z, s) for d in range(N)]
    y_down = [((y + N - d) % N * N + z, s) for d in range(N)]

    def stage_in(n):
        col = pl.multiple_of(at_x(n // 2 % N, n >= 2 * N) * width, 128)
        return pltpu.make_async_copy(gate_up.at[n % 2, pl.ds(col, width)], STAGE.at[n % 2], gsem.at[n % 2])

    def weights(first, last):
        for n in range(first, last):
            stage_in(n).wait()

            @pl.loop(0, width // tok)
            def _(i):
                at = pl.ds(pl.multiple_of(i * tok, tok), tok)
                WG[n // 2, n % 2, at, :] = STAGE[n % 2, at].reshape(tok, 2 * ff)

            if n + 2 < 4 * N:
                stage_in(n + 2).start()

    stage_in(0).start()
    stage_in(1).start()
    loads = []
    for q in range(2 * N):
        col = pl.multiple_of(at_x(q % N, q >= N) * width, 128)
        loads.append(pltpu.make_async_copy(down.at[:, :, pl.ds(col, width)], WD.at[q], wsem.at[q]))
    for load in loads:
        load.start()

    RT[0, 0:top, :] = ids[...].astype(F32)
    RT[0, top : 2 * top, :] = gates[...]

    barrier = pltpu.get_barrier_semaphore()
    friends = z_up[1:] + y_up[1:] + x_at[1:] + [sibling]
    for f in friends:
        pl.semaphore_signal(barrier, inc=1, device_id=f, device_id_type=MESH)
    pl.semaphore_wait(barrier, len(friends))

    copies, done = {}, set()

    def plan(key, src, dst, device):
        i = len(copies)
        copies[key] = pltpu.make_async_remote_copy(
            src_ref=src, dst_ref=dst, send_sem=ssem.at[i], recv_sem=rsem.at[i], device_id=device, device_id_type=MESH
        )

    for p in range(1, N):
        plan(("xa", p), tokens.at[:, A], TA.at[0, back[p]], x_at[p])
        plan(("xo", p), TA.at[0, p], XR.at[back[p] - 1], x_at[p])
    for d in range(1, N):
        plan(("zt", d), tokens.at[:, B], T.at[d], z_up[d])
        plan(("zr", d), RT.at[0], RT.at[d], z_up[d])
        plan(("za", d), TA.at[0], TA.at[d], z_up[d])
        plan(("zo", d), T.at[d], ZR.at[d - 1], z_down[d])
        plan(("zoa", d), TA.at[d], ZA.at[d - 1], z_down[d])
        plan(("yt", d), PL.at[d - 1], XB.at[0, d], y_up[d])
        plan(("yo", d), XB.at[0, d], PL.at[d - 1], y_down[d])
        plan(("ta", d), PA.at[d - 1], XA.at[here, d], y_up[d])
        plan(("ya", d), XA.at[here, d], PA.at[d - 1], y_down[d])
    for g in range(N):
        plan(("r", g), XB.at[0, g], XB.at[1, g], right)
        plan(("l", g), XB.at[0, g], XB.at[2, g], left)
        plan(("rr", g), XB.at[1, g, lo], XB.at[3, g, lo], right)
        plan(("ll", g), XB.at[2, g, hi], XB.at[3, g, hi], left)
        for p in range(N):
            plan(("s", g, p), XB.at[p, g], XB.at[N + p, g], sibling)
        plan(("sa", g), XA.at[here, g], XA.at[there, g], sibling)
        plan(("SA", g), XA.at[there, g], SA.at[:, g], sibling)
        plan(("S", g), XB.at[there, g], SB.at[:, g], sibling)
        plan(("or", g), XB.at[3, g, lo], OP.at[0, g], right)
        plan(("ol", g), XB.at[3, g, hi], OP.at[1, g], left)
        plan(("ir", g, 0), XB.at[2, g, hi], IN.at[0, g, hi], right)
        plan(("il", g, 0), XB.at[1, g, lo], IN.at[1, g, lo], left)
        plan(("ir", g, 1), XB.at[2, g, lo], IN.at[0, g, lo], right)
        plan(("il", g, 1), XB.at[1, g, hi], IN.at[1, g, hi], left)

    def start(*key):
        copies[key].start()

    def sent(*key):
        if key not in done:
            done.add(key)
            copies[key].wait_send()

    def got(*key):
        copies[key].wait_recv()

    for d in (1, 3, 2):
        start("zr", d)
        start("zt", d)
    for p in range(1, N):
        start("xa", p)

    T[0] = tokens[:, B]
    TA[0, 0] = tokens[:, A]
    weights(0, 2)
    for p in range(1, N):
        got("xa", p)
    for d in (1, 3, 2):
        start("za", d)

    line = lax.broadcasted_iota(jnp.int32, (2 * N, tok), 0)
    expert = (2 * (N * ((y + line // 2) % N) + z) + line % 2).astype(F32)
    before = lax.broadcasted_iota(jnp.int32, (tok, tok), 0) < lax.broadcasted_iota(jnp.int32, (tok, tok), 1)
    before = jnp.where(before, 1.0, 0.0).astype(BF16)
    for d in range(N):
        if d:
            got("zr", d)
        named = jnp.zeros((2 * N, tok), F32)
        gate = jnp.zeros((2 * N, tok), F32)
        for k in range(top):
            hit = RT[d, k : k + 1, :] == expert
            named = named + jnp.where(hit, 1.0, 0.0)
            gate = gate + jnp.where(hit, RT[d, top + k : top + k + 1, :], 0.0)
        position = dot(named.astype(BF16), before)
        SLOT[:, d * tok : (d + 1) * tok] = jnp.where(named > 0.0, position + float(d * cap), -1.0)
        GATE[:, d * tok : (d + 1) * tok] = gate

    slot_of = lax.broadcasted_iota(jnp.int32, (half, N * tok), 0).astype(F32)

    def place(g, to):
        for j in range(2):
            i = 2 * g + j
            takes = jnp.where(slot_of == SLOT[i : i + 1, :], 1.0, 0.0).astype(BF16)
            for source, where in to:
                taken = dot(takes, source[...].reshape(N * tok, source.shape[-1]))
                where[j * half : (j + 1) * half, :] = taken.astype(BF16)

    weights(2, 5)
    for d in range(1, N):
        got("zt", d)

    place(0, [(T, XB.at[0, 0])])

    def stage_a(g):
        if g:
            got("yt", g)
        start("r", g)
        start("l", g)
        start("s", g, 0)

    stage_a(0)
    for g in (1, 3, 2):
        place(g, [(T, PL.at[g - 1])])
        start("yt", g)
    for d in range(1, N):
        got("za", d)
    for g in (1, 3, 2):
        place(g, [(TA.at[:, p], PA.at[g - 1, p]) for p in range(N)])
        start("ta", g)
    place(0, [(TA.at[:, p], XA.at[p, 0]) for p in range(N)])

    def stage_b(g):
        got("r", g)
        start("rr", g)
        got("l", g)
        start("ll", g)

    def stage_c(g):
        start("s", g, 1)
        start("s", g, 2)
        if g:
            got("ta", g)
        start("sa", g)
        got("rr", g)
        got("ll", g)
        start("s", g, 3)

    def stage_d(g):
        for p in range(N):
            got("s", g, p)
        got("sa", g)
        ACC[...] = jnp.zeros_like(ACC)

        @pl.loop(0, 2 * N)
        def _(q):
            for j in range(2):
                piece = pl.ds(j * half, half)
                ACC[piece, :] += dot(XB[q, g, piece, :], WG[q, j, B, :]) + dot(XA[q, g, piece, :], WG[q, j, A, :])

        acc = ACC[...]
        HID[...] = (jax.nn.silu(acc[:, :ff]) * acc[:, ff:]).astype(BF16)

        def down_of(q):
            for j in range(2):
                piece = pl.ds(j * half, half)
                result = dot(HID[piece, :], WD[q, j]).astype(BF16)
                XA[q, g, piece, :] = result[:, :a_cols]
                XB[q, g, piece, :] = result[:, a_cols:]

        pl.loop(N, 2 * N)(down_of)
        start("S", g)
        start("SA", g)
        for k in ("r", "l", "rr", "ll", "sa"):
            sent(k, g)
        for p in range(N):
            sent("s", g, p)
        pl.loop(0, N)(down_of)

    def add(n, to, terms):
        @pl.loop(0, n // SUB)
        def _(i):
            at = pl.ds(pl.multiple_of(i * SUB, SUB), SUB)
            total = terms[0][at, :].astype(F32)
            for t in terms[1:]:
                total = total + t[at, :].astype(F32)
            to[at, :] = total.astype(BF16)

    def sum_at(p, g, *more):
        add(rows, XB.at[p, g], [XB.at[p, g], SB.at[p, g], *more])

    def sum_part(p, g, part, *more):
        add(half, XB.at[p, g, part], [XB.at[p, g, part], SB.at[p, g, part], *more])

    def release(g):
        sent("yt", g)
        sent("ta", g)
        pl.semaphore_signal(free.at[g - 1], inc=1, device_id=y_up[g], device_id_type=MESH)

    def stage_e(g):
        got("S", g)
        sum_at(3, g)
        start("or", g)
        start("ol", g)
        sum_part(2, g, hi)
        start("ir", g, 0)
        sum_part(1, g, lo)
        start("il", g, 0)
        got("SA", g)
        for p in range(N):
            add(rows, XA.at[p, g], [XA.at[p, g], SA.at[p, g]])
        if g:
            pl.semaphore_wait(free.at[g - 1], 1)
            start("ya", g)

    def stage_f(g):
        got("or", g)
        sum_part(2, g, lo, OP.at[0, g])
        start("ir", g, 1)
        got("ol", g)
        sum_part(1, g, hi, OP.at[1, g])
        start("il", g, 1)

    def stage_g(g):
        for k in range(2):
            got("ir", g, k)
            got("il", g, k)
        sum_at(0, g, IN.at[0, g], IN.at[1, g])
        if g:
            start("yo", g)

    def combine(g, first, parts):
        @pl.loop(0, N)
        def _(d):
            at = pl.ds(pl.multiple_of(d * tok, tok), tok)
            for j in range(2):
                i = 2 * g + j
                slots = lax.broadcasted_iota(jnp.int32, (half, tok), 0).astype(F32)
                takes = jnp.where(slots == SLOT[i : i + 1, at], GATE[i : i + 1, at], 0.0).astype(BF16)
                for from_, total in parts:
                    product = lax.dot_general(
                        takes, from_[j * half : (j + 1) * half, :], (((0,), (0,)), ((), ())), preferred_element_type=F32
                    )
                    total[at, :] = product if first and j == 0 else total[at, :] + product

    def stage_h(g, first=False):
        if g:
            got("yo", g)
        combine(g, first, [(PL.at[g - 1] if g else XB.at[0, 0], CB)])

    def stage_ha(g, first=False):
        if g:
            got("ya", g)
        combine(g, first, [(PA.at[g - 1, p] if g else XA.at[p, 0], CA.at[p]) for p in range(N)])

    weights(5, 8)
    stage_b(0)
    weights(8, 10)
    stage_a(1)
    stage_a(3)
    stage_c(0)
    weights(10, 14)
    stage_b(1)
    stage_a(2)
    weights(14, 16)
    for load in loads:
        load.wait()
    stage_b(3)
    stage_c(1)
    stage_d(1)
    for g in (1, 3, 2):
        release(g)
    stage_c(3)
    stage_b(2)
    stage_e(1)
    stage_d(3)
    stage_f(1)
    stage_c(2)
    stage_e(3)
    stage_d(2)
    stage_g(1)
    stage_f(3)
    stage_e(2)
    stage_d(0)
    stage_g(3)
    stage_f(2)
    stage_e(0)
    stage_ha(1, True)
    stage_ha(3)
    stage_g(2)
    stage_f(0)
    stage_ha(2)
    stage_ha(0)
    for d in range(1, N):
        sent("za", d)
    for d in range(1, N):
        TA[d] = CA[:, d * tok : (d + 1) * tok, :].astype(BF16)
        start("zoa", d)
    stage_h(1, True)
    stage_h(3)
    total = CA[:, 0:tok, :]
    for d in range(1, N):
        got("zoa", d)
        total = total + ZA[d - 1].astype(F32)
    CA[0, 0:tok, :] = total[0]
    TA[0] = total.astype(BF16)
    for p in range(1, N):
        start("xo", p)
    stage_h(2)
    stage_g(0)
    stage_h(0)
    for d in range(1, N):
        sent("zt", d)
        T[d] = CB[d * tok : (d + 1) * tok, :].astype(BF16)
        start("zo", d)
    total = CA[0, 0:tok, :]
    for p in range(1, N):
        got("xo", p)
        total = total + XR[back[p] - 1].astype(F32)
    out[:, A] = total.astype(BF16)
    total = CB[0:tok, :]
    for d in range(1, N):
        got("zo", d)
        total = total + ZR[d - 1].astype(F32)
    out[:, B] = total.astype(BF16)
    for key in copies:
        sent(*key)


def on_device(tokens, expert_ids, gate_weights, gate_up, down_proj):
    tok, width = tokens.shape
    top = expert_ids.shape[1]
    exp_dev, deep, _, ff = gate_up.shape
    cap = 9 * tok * top // (8 * exp_dev * N * N)
    half = N * cap
    rows = exp_dev * half
    a_cols = 256
    b_cols = width - a_cols
    flops = 2 * N * rows * deep * ff * 3
    n_copies = 11 * (N - 1) + 17 * N
    return pl.pallas_call(
        lambda *refs: kernel(cap, a_cols, *refs),
        out_shape=jax.ShapeDtypeStruct((tok, width), BF16),
        in_specs=[pl.BlockSpec(memory_space=pltpu.VMEM)] * 3 + [pl.BlockSpec(memory_space=pl.ANY)] * 2,
        out_specs=pl.BlockSpec(memory_space=pltpu.VMEM),
        scratch_shapes=[
            pltpu.VMEM((2 * N, N, rows, a_cols), BF16),
            pltpu.VMEM((2 * N, N, rows, b_cols), BF16),
            pltpu.VMEM((N, N, rows, a_cols), BF16),
            pltpu.VMEM((N, N, rows, b_cols), BF16),
            pltpu.VMEM((2, N, half, b_cols), BF16),
            pltpu.VMEM((2, N, rows, b_cols), BF16),
            pltpu.VMEM((N - 1, rows, b_cols), BF16),
            pltpu.VMEM((N - 1, N, rows, a_cols), BF16),
            pltpu.VMEM((N, tok, b_cols), BF16),
            pltpu.VMEM((N, N, tok, a_cols), BF16),
            pltpu.VMEM((N, 2 * top, tok), F32),
            pltpu.VMEM((N - 1, tok, b_cols), BF16),
            pltpu.VMEM((N - 1, N, tok, a_cols), BF16),
            pltpu.VMEM((N - 1, tok, a_cols), BF16),
            pltpu.VMEM((N * tok, b_cols), F32),
            pltpu.VMEM((N, N * tok, a_cols), F32),
            pltpu.VMEM((rows, 2 * ff), F32),
            pltpu.VMEM((rows, ff), BF16),
            pltpu.VMEM((2 * N, N * tok), F32),
            pltpu.VMEM((2 * N, N * tok), F32),
            pltpu.VMEM((2 * N, exp_dev, width, 2 * ff), BF16),
            pltpu.VMEM((2 * N, exp_dev, ff, width), BF16),
            pltpu.VMEM((2, width, 2, ff), BF16),
            pltpu.SemaphoreType.REGULAR((N - 1,)),
            pltpu.SemaphoreType.DMA((2 * N,)),
            pltpu.SemaphoreType.DMA((2,)),
            pltpu.SemaphoreType.DMA((n_copies,)),
            pltpu.SemaphoreType.DMA((n_copies,)),
        ],
        compiler_params=pltpu.CompilerParams(
            collective_id=0, has_side_effects=True, vmem_limit_bytes=62 << 20
        ),
        cost_estimate=pl.CostEstimate(flops=flops, bytes_accessed=24 << 20, transcendentals=0),
    )(tokens, expert_ids.T, gate_weights.T, gate_up, down_proj)


def solution(mesh):
    placed = (
        P("expert", "etensor"),
        P("expert", None),
        P("expert", None),
        P("expert", None, None, "etensor"),
        P("expert", "etensor", None),
    )
    return jax.shard_map(
        on_device, mesh=mesh, in_specs=placed, out_specs=P("expert", "etensor"), check_vma=False
    )
```

time: 186 us -> 147 us (0.79)
  Pallas kernels: 182 us -> 145 us
  other arithmetic: 1.97 us -> 0 us
    pallas_call x1, Pallas kernels: 182 us -> 145 us  [on_device(): pl.pallas_call(lambda *refs: kernel(cap, a_cols, *refs), out_shape=jax.Sh...]
where the time goes in v4:
time: 147 us
  Pallas kernels  145 us (99%)
  local copies, waits for them, and re-layouts  1.65 us (1%)
    pallas_call x1, Pallas kernels, on_device(): pl.pallas_call(lambda *refs: kernel(cap, a_cols, *refs), out_shape=jax.Sh...  145 us

profile of v4, /device:TPU:1, one launch (start us, length us, event | category | flops | bytes accessed | tf_op | source)
XLA Modules:
  0.0 146.5 jit_solution(6392740635356192003)
XLA Ops:
  0.0 144.9 %shard_map.55 = bf16[128,896]{1,0:T(8,128)(2,1)} custom-call(bf16[128,896]{1,0:T(8,128)(2,1)} %refs_0_.1, s32[8,128]{1,0:T(8,128)} %bitcast.2, f32[8,128]{1,0:T(8,128)} %bitcast.3, bf16[2,7168,2,256]{3,2,1,0:T(2,128)(2,1)} %refs_3_.1, bf16[2,256,7168]{2,1,0:T(8,128)(2,1)} %refs_4_.1), custom_call_target="tpu_custom_call" | custom-call | flops 12683575296 | bytes 25165824 | tf_op jit(solution)/shard_map/pallas_call | solution.py:399
  144.9 1.6 %copy.7 = bf16[128,896]{1,0:T(8,128)(2,1)} copy(bf16[128,896]{1,0:T(8,128)(2,1)} %shard_map.55) | data formatting | bytes 458752

commit v5 on v4

--- a/solution.py
+++ b/solution.py
@@ -132,10 +132,6 @@
     T[0] = tokens[:, B]
     TA[0, 0] = tokens[:, A]
     weights(0, 2)
-    for p in range(1, N):
-        got("xa", p)
-    for d in (1, 3, 2):
-        start("za", d)
 
     line = lax.broadcasted_iota(jnp.int32, (2 * N, tok), 0)
     expert = (2 * (N * ((y + line // 2) % N) + z) + line % 2).astype(F32)
@@ -167,6 +163,10 @@
     weights(2, 5)
     for d in range(1, N):
         got("zt", d)
+    for p in range(1, N):
+        got("xa", p)
+    for d in (1, 3, 2):
+        start("za", d)
 
     place(0, [(T, XB.at[0, 0])])
 
@@ -181,12 +181,6 @@
     for g in (1, 3, 2):
         place(g, [(T, PL.at[g - 1])])
         start("yt", g)
-    for d in range(1, N):
-        got("za", d)
-    for g in (1, 3, 2):
-        place(g, [(TA.at[:, p], PA.at[g - 1, p]) for p in range(N)])
-        start("ta", g)
-    place(0, [(TA.at[:, p], XA.at[p, 0]) for p in range(N)])
 
     def stage_b(g):
         got("r", g)
@@ -311,16 +305,21 @@
             got("ya", g)
         combine(g, first, [(PA.at[g - 1, p] if g else XA.at[p, 0], CA.at[p]) for p in range(N)])
 
-    weights(5, 8)
+    weights(5, 10)
     stage_b(0)
-    weights(8, 10)
     stage_a(1)
     stage_a(3)
+    for d in range(1, N):
+        got("za", d)
+    for g in (1, 3, 2):
+        place(g, [(TA.at[:, p], PA.at[g - 1, p]) for p in range(N)])
+        start("ta", g)
+    place(0, [(TA.at[:, p], XA.at[p, 0]) for p in range(N)])
     stage_c(0)
-    weights(10, 14)
+    weights(10, 13)
     stage_b(1)
     stage_a(2)
-    weights(14, 16)
+    weights(13, 16)
     for load in loads:
         load.wait()
     stage_b(3)
@@ -342,20 +341,26 @@
     stage_d(0)
     stage_g(3)
     stage_f(2)
-    stage_e(0)
     stage_ha(1, True)
     stage_ha(3)
-    stage_g(2)
-    stage_f(0)
+    stage_e(0)
     stage_ha(2)
     stage_ha(0)
     for d in range(1, N):
         sent("za", d)
-    for d in range(1, N):
+    for d in (1, 3, 2):
         TA[d] = CA[:, d * tok : (d + 1) * tok, :].astype(BF16)
         start("zoa", d)
     stage_h(1, True)
+    stage_f(0)
+    stage_g(2)
     stage_h(3)
+    stage_h(2)
+    stage_g(0)
+    stage_h(0)
+    for d in (1, 3, 2):
+        T[d] = CB[d * tok : (d + 1) * tok, :].astype(BF16)
+        start("zo", d)
     total = CA[:, 0:tok, :]
     for d in range(1, N):
         got("zoa", d)
@@ -364,23 +369,16 @@
     TA[0] = total.astype(BF16)
     for p in range(1, N):
         start("xo", p)
-    stage_h(2)
-    stage_g(0)
-    stage_h(0)
-    for d in range(1, N):
-        sent("zt", d)
-        T[d] = CB[d * tok : (d + 1) * tok, :].astype(BF16)
-        start("zo", d)
+    total = CB[0:tok, :]
+    for d in range(1, N):
+        got("zo", d)
+        total = total + ZR[d - 1].astype(F32)
+    out[:, B] = total.astype(BF16)
     total = CA[0, 0:tok, :]
     for p in range(1, N):
         got("xo", p)
         total = total + XR[back[p] - 1].astype(F32)
     out[:, A] = total.astype(BF16)
-    total = CB[0:tok, :]
-    for d in range(1, N):
-        got("zo", d)
-        total = total + ZR[d - 1].astype(F32)
-    out[:, B] = total.astype(BF16)
     for key in copies:
         sent(*key)
 

time: 147 us -> 138 us (0.939); the launches traced: 147 us -> 136 us
  Pallas kernels: 145 us -> 134 us
    pallas_call x1, Pallas kernels: 145 us -> 134 us  [on_device(): pl.pallas_call(lambda *refs: kernel(cap, a_cols, *refs), out_shape=jax.Sh...]
where the time goes in v5:
time: 138 us; the launch traced here: 136 us
  Pallas kernels  134 us (97%)
  local copies, waits for them, and re-layouts  1.65 us (1%)
    pallas_call x1, Pallas kernels, on_device(): pl.pallas_call(lambda *refs: kernel(cap, a_cols, *refs), out_shape=jax.Sh...  134 us

profile of v5, /device:TPU:1, one launch (start us, length us, event | category | flops | bytes accessed | tf_op | source)
XLA Modules:
  0.0 136.0 jit_solution(16053452100186311860)
XLA Ops:
  0.0 134.3 %shard_map.55 = bf16[128,896]{1,0:T(8,128)(2,1)} custom-call(bf16[128,896]{1,0:T(8,128)(2,1)} %refs_0_.1, s32[8,128]{1,0:T(8,128)} %bitcast.2, f32[8,128]{1,0:T(8,128)} %bitcast.3, bf16[2,7168,2,256]{3,2,1,0:T(2,128)(2,1)} %refs_3_.1, bf16[2,256,7168]{2,1,0:T(8,128)(2,1)} %refs_4_.1), custom_call_target="tpu_custom_call" | custom-call | flops 12683575296 | bytes 25165824 | tf_op jit(solution)/shard_map/pallas_call | solution.py:397
  134.3 1.6 %copy.7 = bf16[128,896]{1,0:T(8,128)(2,1)} copy(bf16[128,896]{1,0:T(8,128)(2,1)} %shard_map.55) | data formatting | bytes 458752

commit v6 on v5

--- a/solution.py
+++ b/solution.py
@@ -322,6 +322,7 @@
     weights(13, 16)
     for load in loads:
         load.wait()
+    stage_d(0)
     stage_b(3)
     stage_c(1)
     stage_d(1)
@@ -338,7 +339,6 @@
     stage_g(1)
     stage_f(3)
     stage_e(2)
-    stage_d(0)
     stage_g(3)
     stage_f(2)
     stage_ha(1, True)

time: 138 us -> 138 us (level); the launches traced: 136 us -> 138 us
  Pallas kernels: 134 us -> 136 us
    pallas_call x1, Pallas kernels: 134 us -> 136 us  [on_device(): pl.pallas_call(lambda *refs: kernel(cap, a_cols, *refs), out_shape=jax.Sh...]
where the time goes in v6:
time: 138 us
  Pallas kernels  136 us (99%)
  local copies, waits for them, and re-layouts  1.65 us (1%)
    pallas_call x1, Pallas kernels, on_device(): pl.pallas_call(lambda *refs: kernel(cap, a_cols, *refs), out_shape=jax.Sh...  136 us

profile of v6, /device:TPU:1, one launch (start us, length us, event | category | flops | bytes accessed | tf_op | source)
XLA Modules:
  0.0 137.7 jit_solution(8607548085531348736)
XLA Ops:
  0.0 136.0 %shard_map.55 = bf16[128,896]{1,0:T(8,128)(2,1)} custom-call(bf16[128,896]{1,0:T(8,128)(2,1)} %refs_0_.1, s32[8,128]{1,0:T(8,128)} %bitcast.2, f32[8,128]{1,0:T(8,128)} %bitcast.3, bf16[2,7168,2,256]{3,2,1,0:T(2,128)(2,1)} %refs_3_.1, bf16[2,256,7168]{2,1,0:T(8,128)(2,1)} %refs_4_.1), custom_call_target="tpu_custom_call" | custom-call | flops 12683575296 | bytes 25165824 | tf_op jit(solution)/shard_map/pallas_call | solution.py:397
  136.0 1.6 %copy.7 = bf16[128,896]{1,0:T(8,128)(2,1)} copy(bf16[128,896]{1,0:T(8,128)(2,1)} %shard_map.55) | data formatting | bytes 458752
